TPU v7x, 32 devices: a whole 2x2x4 slice. The times are simulated.
32 devices in a mesh: wide: 8 (over y, x, core), narrow: 4 (over z).
Axes of the slice: x: 2, y: 2, z: 4, core: 2. Of those that a mesh axis runs over, the one named last changes fastest.
Arguments:
- hidden_in: bfloat16 [131072, 768], P(('wide', 'narrow')), may hold values from -6 to 6
- lengths: int32 [256], P(('wide', 'narrow')), may hold values from 16 to 512, as said below
- labels: int32 [256], P(('wide', 'narrow')), may hold values from 0 to 2
- qkv_weight: bfloat16 [768, 2304], replicated, may hold values from -0.21875 to 0.21875
- qkv_bias: float32 [2304], replicated, may hold values from -4 to 4
- out_weight: bfloat16 [768, 768], replicated, may hold values from -0.875 to 0.875
- out_bias: float32 [768], replicated, may hold values from -4 to 4
- attention_gain: float32 [768], replicated, may hold values from 0.5 to 1.5
- attention_shift: float32 [768], replicated, may hold values from -4 to 4
- up_weight: bfloat16 [768, 3072], replicated, may hold values from -0.21875 to 0.21875
- up_bias: float32 [3072], replicated, may hold values from -4 to 4
- down_weight: bfloat16 [3072, 768], replicated, may hold values from -0.109375 to 0.109375
- down_bias: float32 [768], replicated, may hold values from -4 to 4
- output_gain: float32 [768], replicated, may hold values from 0.5 to 1.5
- output_shift: float32 [768], replicated, may hold values from -4 to 4
- pooler_weight: bfloat16 [768, 768], replicated, may hold values from -0.21875 to 0.21875
- pooler_bias: float32 [768], replicated, may hold values from -6 to 6
- ramp_weight: float32 [768, 3], replicated, may hold values from -1.5 to 1.5
- ramp_bias: float32 [3], replicated, may hold values from -6 to 6
Outputs:
- hidden_out: bfloat16 [131072, 768], P(('wide', 'narrow'))
- logits: float32 [256, 3], P(('wide', 'narrow'))
- grad_pooler_weight: float32 [768, 768], replicated
- grad_pooler_bias: float32 [768], replicated
- grad_ramp_weight: float32 [768, 3], replicated
- grad_ramp_bias: float32 [3], replicated
- entropy: float32 [], replicated
Inputs may be any that keep to these rules, and one draw needn't show every extreme that they name: `lengths`: every sequence has at least 16 tokens; in every draw some sequence fills its slot of 512.
All inputs are finite; a program needn't handle non-finite values.
Results may differ from a plain program's by a relative error of at most 0.0075.
Values sent between devices are 32-bit elements; how exact they have to be, the bound alone decides.
No kernel may reach another device: no remote copies, remote signals or barrier semaphores. Data moves between devices by JAX's collectives and lax.ppermute only.
A program may use at most 128 MiB of HBM per device.

v0:
```python
import jax
import jax.numpy as jnp
from jax import lax
from jax.sharding import PartitionSpec as P

D = 768
HEADS = 12
HEAD_DIM = 64
CLASSES = 3


HIGHEST = lax.Precision.HIGHEST


def matmul(left, right):
    return jnp.dot(left, right, precision=HIGHEST, preferred_element_type=jnp.float32)


def layer_norm(values, gain, shift):
    center = values - jnp.mean(values, axis=-1, keepdims=True)
    spread = jnp.mean(center * center, axis=-1, keepdims=True)
    return center * lax.rsqrt(spread + 1e-12) * gain + shift


def encode(tokens, length, weights):
    (
        qkv_weight,
        qkv_bias,
        out_weight,
        out_bias,
        attention_gain,
        attention_shift,
        up_weight,
        up_bias,
        down_weight,
        down_bias,
        output_gain,
        output_shift,
    ) = weights
    rows = tokens.shape[0]
    projected = jnp.dot(tokens, qkv_weight, preferred_element_type=jnp.float32) + qkv_bias
    queries = projected[:, :D].astype(jnp.bfloat16).reshape(rows, HEADS, HEAD_DIM)
    key_rows = projected[:, D : 2 * D].astype(jnp.bfloat16).reshape(rows, HEADS, HEAD_DIM)
    value_rows = projected[:, 2 * D :].astype(jnp.bfloat16).reshape(rows, HEADS, HEAD_DIM)
    scores = jnp.einsum(
        "qhd,khd->hqk", queries, key_rows, preferred_element_type=jnp.float32
    ) * HEAD_DIM ** (-0.5)
    positions = jnp.arange(rows)
    visible = positions[None, None, :] < length
    scores = jnp.where(visible, scores, jnp.float32(-1000000000.0))
    row_max = jnp.max(scores, axis=-1, keepdims=True)
    weights_exp = jnp.exp(scores - row_max)
    attention = (weights_exp / jnp.sum(weights_exp, axis=-1, keepdims=True)).astype(jnp.bfloat16)
    context = jnp.einsum("hqk,khd->qhd", attention, value_rows, preferred_element_type=jnp.float32)
    context = context.reshape(rows, D).astype(jnp.bfloat16)
    attended = jnp.dot(context, out_weight, preferred_element_type=jnp.float32) + out_bias
    after_attention = layer_norm(
        tokens.astype(jnp.float32) + attended, attention_gain, attention_shift
    )
    expanded = (
        jnp.dot(after_attention.astype(jnp.bfloat16), up_weight, preferred_element_type=jnp.float32)
        + up_bias
    )
    active = jax.nn.gelu(expanded, approximate=False).astype(jnp.bfloat16)
    second = jnp.dot(active, down_weight, preferred_element_type=jnp.float32) + down_bias
    return layer_norm(after_attention + second, output_gain, output_shift).astype(jnp.bfloat16)


def local(
    hidden_in,
    lengths,
    labels,
    qkv_weight,
    qkv_bias,
    out_weight,
    out_bias,
    attention_gain,
    attention_shift,
    up_weight,
    up_bias,
    down_weight,
    down_bias,
    output_gain,
    output_shift,
    pooler_weight,
    pooler_bias,
    ramp_weight,
    ramp_bias,
):
    weights = (
        qkv_weight,
        qkv_bias,
        out_weight,
        out_bias,
        attention_gain,
        attention_shift,
        up_weight,
        up_bias,
        down_weight,
        down_bias,
        output_gain,
        output_shift,
    )
    slot_count = lengths.shape[0]
    sequences = hidden_in.reshape(slot_count, -1, hidden_in.shape[1])
    encoded = lax.map(lambda carried: encode(carried[0], carried[1], weights), (sequences, lengths))
    hidden_out = encoded.reshape(hidden_in.shape)
    leading = encoded[:, 0, :]
    pooled = jnp.tanh(
        jnp.dot(leading, pooler_weight, preferred_element_type=jnp.float32) + pooler_bias
    )
    logits = matmul(pooled, ramp_weight) + ramp_bias
    onehot = (labels[:, None] == jnp.arange(CLASSES)[None, :]).astype(jnp.float32)
    dlogits = jax.nn.softmax(logits, axis=1) - onehot
    grad_ramp_weight = matmul(pooled.T, dlogits)
    grad_ramp_bias = jnp.sum(dlogits, axis=0)
    pooled_grad = (matmul(dlogits, ramp_weight.T) * (1.0 - pooled * pooled)).astype(jnp.bfloat16)
    grad_pooler_weight = jnp.dot(leading.T, pooled_grad, preferred_element_type=jnp.float32)
    grad_pooler_bias = jnp.sum(pooled_grad.astype(jnp.float32), axis=0)
    log_probs = jax.nn.log_softmax(logits, axis=1)
    row_entropy = -jnp.sum(jnp.exp(log_probs) * log_probs, axis=1)
    length_float = lengths.astype(jnp.float32)
    entropy_sum = jnp.sum(length_float * row_entropy)
    length_count = jnp.sum(length_float)
    totals = lax.psum(
        (
            grad_pooler_weight,
            grad_ramp_weight,
            grad_pooler_bias,
            grad_ramp_bias,
            entropy_sum,
            length_count,
        ),
        ("wide", "narrow"),
    )
    (
        grad_pooler_weight,
        grad_ramp_weight,
        grad_pooler_bias,
        grad_ramp_bias,
        entropy_sum,
        length_count,
    ) = totals
    entropy = entropy_sum / length_count
    return (
        hidden_out,
        logits,
        grad_pooler_weight,
        grad_pooler_bias,
        grad_ramp_weight,
        grad_ramp_bias,
        entropy,
    )


def solution(mesh):
    placed = (
        P(("wide", "narrow"), None),
        P(("wide", "narrow")),
        P(("wide", "narrow")),
        P(),
        P(),
        P(),
        P(),
        P(),
        P(),
        P(),
        P(),
        P(),
        P(),
        P(),
        P(),
        P(),
        P(),
        P(),
        P(),
    )
    return jax.shard_map(
        local,
        mesh=mesh,
        in_specs=placed,
        out_specs=(
            P(("wide", "narrow"), None),
            P(("wide", "narrow"), None),
            P(),
            P(),
            P(),
            P(),
            P(),
        ),
        check_vma=False,
    )
```

profile of v0, /device:TPU:0, one launch (start us, length us, event | category | flops | bytes accessed | tf_op | source)
XLA Modules:
  0.0 570.2 jit_solution(17959045917789183911)
XLA Ops:
  7.2 404.2 %while.10 = (s32[]{:T(128)}, bf16[8,512,768]{2,1,0:T(8,128)(2,1)}, bf16[8,512,768]{2,1,0:T(8,128)(2,1)}, bf16[768,2304]{1,0:T(8,128)(2,1)}, f32[2304]{0:T(1024)}...) while((s32[]{:T(128)}, bf16[8,512,768]{2,1,0:T(8,128)(2,1)}, ...), condition=%wide.region_7.8_spmd, body=%wide.region_0.7_spmd.sunk | while | flops 8189118464 | bytes 78111304 | solution.py:106
  7.2 4.3 fusion.127
  11.7 1.2 copy.40
  14.4 10.7 %fusion.129 = (f32[12,512]{1,0:T(8,128)S(1)}, f32[12,512,512]{1,2,0:T(8,128)}) fusion(pred[512]{0:T(512)(128)(4,1)S(1)} %iota_compare_fusion.3, bf16[512,12,64]{0,2,1:T(8,128)(2,1)} %bitcast.69, bf16[512,12,64]{0,2,1:T(8,128)(2,1)S(1)} %bitcast.70), kind=kOutput, calls=%fused_computation.103.clone.1 | convolution fusion | flops 415236608 | bytes 14180864 | tf_op jit(solution)/shard_map/while/body/eval_jaxpr/sub | solution.py:52
  25.4 5.9 %fusion.130 = bf16[12,64,512]{2,1,0:T(8,128)(2,1)S(1)} fusion(bf16[512,12,64]{0,2,1:T(8,128)(2,1)S(1)} %bitcast.71, f32[12,512,512]{1,2,0:T(8,128)} %get-tuple-element.254, f32[12,512]{1,0:T(8,128)S(1)} %get-tuple-element.255), kind=kOutput, calls=%fused_computation.37.clone.1 | convolution fusion | flops 409337856 | bytes 14180352 | tf_op jit(solution)/shard_map/while/body/eval_jaxpr/hqk,khd->qhd/dot_general | solution.py:54
  31.3 2.1 fusion.131
  34.6 21.7 %fusion.132 = (f32[512]{0:T(512)S(1)}, f32[512,768]{1,0:T(8,128)S(1)}) fusion(f32[768]{0:T(1024)S(1)} %copy-done.15, bf16[3072,768]{1,0:T(8,128)(2,1)} %get-tuple-element.306, bf16[768,3072]{1,0:T(8,128)(2,1)} %get-tuple-element.304, f32[3072]{0:T(1024)S(1)} %copy-done.11, f32[512,768]{1,0:T(8,128)} %copy-done.1, f32[768]{0:T(1024)S(1)} %copy-done.14, ...), kind=kOutput, calls=%fused_computation.105.clone.1 | convolution fusion | flops 4940365312 | bytes 12610560 | tf_op jit(solution)/shard_map/while/body/eval_jaxpr/dot_general | solution.py:65
  56.7 1.2 fusion.133
  57.9 4.2 fusion.127
  62.2 1.2 copy.40
  64.9 10.6 %fusion.129 = (f32[12,512]{1,0:T(8,128)S(1)}, f32[12,512,512]{1,2,0:T(8,128)}) fusion(pred[512]{0:T(512)(128)(4,1)S(1)} %iota_compare_fusion.3, bf16[512,12,64]{0,2,1:T(8,128)(2,1)} %bitcast.69, bf16[512,12,64]{0,2,1:T(8,128)(2,1)S(1)} %bitcast.70), kind=kOutput, calls=%fused_computation.103.clone.1 | convolution fusion | flops 415236608 | bytes 14180864 | tf_op jit(solution)/shard_map/while/body/eval_jaxpr/sub | solution.py:52
  75.9 5.9 %fusion.130 = bf16[12,64,512]{2,1,0:T(8,128)(2,1)S(1)} fusion(bf16[512,12,64]{0,2,1:T(8,128)(2,1)S(1)} %bitcast.71, f32[12,512,512]{1,2,0:T(8,128)} %get-tuple-element.254, f32[12,512]{1,0:T(8,128)S(1)} %get-tuple-element.255), kind=kOutput, calls=%fused_computation.37.clone.1 | convolution fusion | flops 409337856 | bytes 14180352 | tf_op jit(solution)/shard_map/while/body/eval_jaxpr/hqk,khd->qhd/dot_general | solution.py:54
  81.9 2.1 fusion.131
  84.3 0.8 copy-done.1
  85.1 21.7 %fusion.132 = (f32[512]{0:T(512)S(1)}, f32[512,768]{1,0:T(8,128)S(1)}) fusion(f32[768]{0:T(1024)S(1)} %copy-done.15, bf16[3072,768]{1,0:T(8,128)(2,1)} %get-tuple-element.306, bf16[768,3072]{1,0:T(8,128)(2,1)} %get-tuple-element.304, f32[3072]{0:T(1024)S(1)} %copy-done.11, f32[512,768]{1,0:T(8,128)} %copy-done.1, f32[768]{0:T(1024)S(1)} %copy-done.14, ...), kind=kOutput, calls=%fused_computation.105.clone.1 | convolution fusion | flops 4940365312 | bytes 12610560 | tf_op jit(solution)/shard_map/while/body/eval_jaxpr/dot_general | solution.py:65
  107.2 1.2 fusion.133
  108.4 4.2 fusion.127
  112.8 1.2 copy.40
  115.5 10.6 %fusion.129 = (f32[12,512]{1,0:T(8,128)S(1)}, f32[12,512,512]{1,2,0:T(8,128)}) fusion(pred[512]{0:T(512)(128)(4,1)S(1)} %iota_compare_fusion.3, bf16[512,12,64]{0,2,1:T(8,128)(2,1)} %bitcast.69, bf16[512,12,64]{0,2,1:T(8,128)(2,1)S(1)} %bitcast.70), kind=kOutput, calls=%fused_computation.103.clone.1 | convolution fusion | flops 415236608 | bytes 14180864 | tf_op jit(solution)/shard_map/while/body/eval_jaxpr/sub | solution.py:52
  126.4 5.9 %fusion.130 = bf16[12,64,512]{2,1,0:T(8,128)(2,1)S(1)} fusion(bf16[512,12,64]{0,2,1:T(8,128)(2,1)S(1)} %bitcast.71, f32[12,512,512]{1,2,0:T(8,128)} %get-tuple-element.254, f32[12,512]{1,0:T(8,128)S(1)} %get-tuple-element.255), kind=kOutput, calls=%fused_computation.37.clone.1 | convolution fusion | flops 409337856 | bytes 14180352 | tf_op jit(solution)/shard_map/while/body/eval_jaxpr/hqk,khd->qhd/dot_general | solution.py:54
  132.4 2.1 fusion.131
  135.6 21.7 %fusion.132 = (f32[512]{0:T(512)S(1)}, f32[512,768]{1,0:T(8,128)S(1)}) fusion(f32[768]{0:T(1024)S(1)} %copy-done.15, bf16[3072,768]{1,0:T(8,128)(2,1)} %get-tuple-element.306, bf16[768,3072]{1,0:T(8,128)(2,1)} %get-tuple-element.304, f32[3072]{0:T(1024)S(1)} %copy-done.11, f32[512,768]{1,0:T(8,128)} %copy-done.1, f32[768]{0:T(1024)S(1)} %copy-done.14, ...), kind=kOutput, calls=%fused_computation.105.clone.1 | convolution fusion | flops 4940365312 | bytes 12610560 | tf_op jit(solution)/shard_map/while/body/eval_jaxpr/dot_general | solution.py:65
  157.7 1.2 fusion.133
  158.9 4.2 fusion.127
  163.3 1.2 copy.40
  166.0 10.6 %fusion.129 = (f32[12,512]{1,0:T(8,128)S(1)}, f32[12,512,512]{1,2,0:T(8,128)}) fusion(pred[512]{0:T(512)(128)(4,1)S(1)} %iota_compare_fusion.3, bf16[512,12,64]{0,2,1:T(8,128)(2,1)} %bitcast.69, bf16[512,12,64]{0,2,1:T(8,128)(2,1)S(1)} %bitcast.70), kind=kOutput, calls=%fused_computation.103.clone.1 | convolution fusion | flops 415236608 | bytes 14180864 | tf_op jit(solution)/shard_map/while/body/eval_jaxpr/sub | solution.py:52
  176.9 5.9 %fusion.130 = bf16[12,64,512]{2,1,0:T(8,128)(2,1)S(1)} fusion(bf16[512,12,64]{0,2,1:T(8,128)(2,1)S(1)} %bitcast.71, f32[12,512,512]{1,2,0:T(8,128)} %get-tuple-element.254, f32[12,512]{1,0:T(8,128)S(1)} %get-tuple-element.255), kind=kOutput, calls=%fused_computation.37.clone.1 | convolution fusion | flops 409337856 | bytes 14180352 | tf_op jit(solution)/shard_map/while/body/eval_jaxpr/hqk,khd->qhd/dot_general | solution.py:54
  182.9 2.1 fusion.131
  185.3 0.8 copy-done.1
  186.1 21.7 %fusion.132 = (f32[512]{0:T(512)S(1)}, f32[512,768]{1,0:T(8,128)S(1)}) fusion(f32[768]{0:T(1024)S(1)} %copy-done.15, bf16[3072,768]{1,0:T(8,128)(2,1)} %get-tuple-element.306, bf16[768,3072]{1,0:T(8,128)(2,1)} %get-tuple-element.304, f32[3072]{0:T(1024)S(1)} %copy-done.11, f32[512,768]{1,0:T(8,128)} %copy-done.1, f32[768]{0:T(1024)S(1)} %copy-done.14, ...), kind=kOutput, calls=%fused_computation.105.clone.1 | convolution fusion | flops 4940365312 | bytes 12610560 | tf_op jit(solution)/shard_map/while/body/eval_jaxpr/dot_general | solution.py:65
  208.2 1.2 fusion.133
  209.4 4.2 fusion.127
  213.8 1.2 copy.40
  216.5 10.6 %fusion.129 = (f32[12,512]{1,0:T(8,128)S(1)}, f32[12,512,512]{1,2,0:T(8,128)}) fusion(pred[512]{0:T(512)(128)(4,1)S(1)} %iota_compare_fusion.3, bf16[512,12,64]{0,2,1:T(8,128)(2,1)} %bitcast.69, bf16[512,12,64]{0,2,1:T(8,128)(2,1)S(1)} %bitcast.70), kind=kOutput, calls=%fused_computation.103.clone.1 | convolution fusion | flops 415236608 | bytes 14180864 | tf_op jit(solution)/shard_map/while/body/eval_jaxpr/sub | solution.py:52
  227.5 5.9 %fusion.130 = bf16[12,64,512]{2,1,0:T(8,128)(2,1)S(1)} fusion(bf16[512,12,64]{0,2,1:T(8,128)(2,1)S(1)} %bitcast.71, f32[12,512,512]{1,2,0:T(8,128)} %get-tuple-element.254, f32[12,512]{1,0:T(8,128)S(1)} %get-tuple-element.255), kind=kOutput, calls=%fused_computation.37.clone.1 | convolution fusion | flops 409337856 | bytes 14180352 | tf_op jit(solution)/shard_map/while/body/eval_jaxpr/hqk,khd->qhd/dot_general | solution.py:54
  233.4 2.1 fusion.131
  236.7 21.7 %fusion.132 = (f32[512]{0:T(512)S(1)}, f32[512,768]{1,0:T(8,128)S(1)}) fusion(f32[768]{0:T(1024)S(1)} %copy-done.15, bf16[3072,768]{1,0:T(8,128)(2,1)} %get-tuple-element.306, bf16[768,3072]{1,0:T(8,128)(2,1)} %get-tuple-element.304, f32[3072]{0:T(1024)S(1)} %copy-done.11, f32[512,768]{1,0:T(8,128)} %copy-done.1, f32[768]{0:T(1024)S(1)} %copy-done.14, ...), kind=kOutput, calls=%fused_computation.105.clone.1 | convolution fusion | flops 4940365312 | bytes 12610560 | tf_op jit(solution)/shard_map/while/body/eval_jaxpr/dot_general | solution.py:65
  258.7 1.2 fusion.133
  259.9 4.2 fusion.127
  264.3 1.2 copy.40
  267.0 10.6 %fusion.129 = (f32[12,512]{1,0:T(8,128)S(1)}, f32[12,512,512]{1,2,0:T(8,128)}) fusion(pred[512]{0:T(512)(128)(4,1)S(1)} %iota_compare_fusion.3, bf16[512,12,64]{0,2,1:T(8,128)(2,1)} %bitcast.69, bf16[512,12,64]{0,2,1:T(8,128)(2,1)S(1)} %bitcast.70), kind=kOutput, calls=%fused_computation.103.clone.1 | convolution fusion | flops 415236608 | bytes 14180864 | tf_op jit(solution)/shard_map/while/body/eval_jaxpr/sub | solution.py:52
  278.0 5.9 %fusion.130 = bf16[12,64,512]{2,1,0:T(8,128)(2,1)S(1)} fusion(bf16[512,12,64]{0,2,1:T(8,128)(2,1)S(1)} %bitcast.71, f32[12,512,512]{1,2,0:T(8,128)} %get-tuple-element.254, f32[12,512]{1,0:T(8,128)S(1)} %get-tuple-element.255), kind=kOutput, calls=%fused_computation.37.clone.1 | convolution fusion | flops 409337856 | bytes 14180352 | tf_op jit(solution)/shard_map/while/body/eval_jaxpr/hqk,khd->qhd/dot_general | solution.py:54
  283.9 2.1 fusion.131
  287.2 21.7 %fusion.132 = (f32[512]{0:T(512)S(1)}, f32[512,768]{1,0:T(8,128)S(1)}) fusion(f32[768]{0:T(1024)S(1)} %copy-done.15, bf16[3072,768]{1,0:T(8,128)(2,1)} %get-tuple-element.306, bf16[768,3072]{1,0:T(8,128)(2,1)} %get-tuple-element.304, f32[3072]{0:T(1024)S(1)} %copy-done.11, f32[512,768]{1,0:T(8,128)} %copy-done.1, f32[768]{0:T(1024)S(1)} %copy-done.14, ...), kind=kOutput, calls=%fused_computation.105.clone.1 | convolution fusion | flops 4940365312 | bytes 12610560 | tf_op jit(solution)/shard_map/while/body/eval_jaxpr/dot_general | solution.py:65
  309.2 1.2 fusion.133
  310.4 4.2 fusion.127
  314.8 1.2 copy.40
  317.5 10.6 %fusion.129 = (f32[12,512]{1,0:T(8,128)S(1)}, f32[12,512,512]{1,2,0:T(8,128)}) fusion(pred[512]{0:T(512)(128)(4,1)S(1)} %iota_compare_fusion.3, bf16[512,12,64]{0,2,1:T(8,128)(2,1)} %bitcast.69, bf16[512,12,64]{0,2,1:T(8,128)(2,1)S(1)} %bitcast.70), kind=kOutput, calls=%fused_computation.103.clone.1 | convolution fusion | flops 415236608 | bytes 14180864 | tf_op jit(solution)/shard_map/while/body/eval_jaxpr/sub | solution.py:52
  328.5 5.9 %fusion.130 = bf16[12,64,512]{2,1,0:T(8,128)(2,1)S(1)} fusion(bf16[512,12,64]{0,2,1:T(8,128)(2,1)S(1)} %bitcast.71, f32[12,512,512]{1,2,0:T(8,128)} %get-tuple-element.254, f32[12,512]{1,0:T(8,128)S(1)} %get-tuple-element.255), kind=kOutput, calls=%fused_computation.37.clone.1 | convolution fusion | flops 409337856 | bytes 14180352 | tf_op jit(solution)/shard_map/while/body/eval_jaxpr/hqk,khd->qhd/dot_general | solution.py:54
  334.5 2.1 fusion.131
  337.7 21.7 %fusion.132 = (f32[512]{0:T(512)S(1)}, f32[512,768]{1,0:T(8,128)S(1)}) fusion(f32[768]{0:T(1024)S(1)} %copy-done.15, bf16[3072,768]{1,0:T(8,128)(2,1)} %get-tuple-element.306, bf16[768,3072]{1,0:T(8,128)(2,1)} %get-tuple-element.304, f32[3072]{0:T(1024)S(1)} %copy-done.11, f32[512,768]{1,0:T(8,128)} %copy-done.1, f32[768]{0:T(1024)S(1)} %copy-done.14, ...), kind=kOutput, calls=%fused_computation.105.clone.1 | convolution fusion | flops 4940365312 | bytes 12610560 | tf_op jit(solution)/shard_map/while/body/eval_jaxpr/dot_general | solution.py:65
  359.8 1.2 fusion.133
  361.0 4.2 fusion.127
  365.3 1.2 copy.40
  368.0 10.6 %fusion.129 = (f32[12,512]{1,0:T(8,128)S(1)}, f32[12,512,512]{1,2,0:T(8,128)}) fusion(pred[512]{0:T(512)(128)(4,1)S(1)} %iota_compare_fusion.3, bf16[512,12,64]{0,2,1:T(8,128)(2,1)} %bitcast.69, bf16[512,12,64]{0,2,1:T(8,128)(2,1)S(1)} %bitcast.70), kind=kOutput, calls=%fused_computation.103.clone.1 | convolution fusion | flops 415236608 | bytes 14180864 | tf_op jit(solution)/shard_map/while/body/eval_jaxpr/sub | solution.py:52
  379.0 5.9 %fusion.130 = bf16[12,64,512]{2,1,0:T(8,128)(2,1)S(1)} fusion(bf16[512,12,64]{0,2,1:T(8,128)(2,1)S(1)} %bitcast.71, f32[12,512,512]{1,2,0:T(8,128)} %get-tuple-element.254, f32[12,512]{1,0:T(8,128)S(1)} %get-tuple-element.255), kind=kOutput, calls=%fused_computation.37.clone.1 | convolution fusion | flops 409337856 | bytes 14180352 | tf_op jit(solution)/shard_map/while/body/eval_jaxpr/hqk,khd->qhd/dot_general | solution.py:54
  385.0 2.1 fusion.131
  388.2 21.7 %fusion.132 = (f32[512]{0:T(512)S(1)}, f32[512,768]{1,0:T(8,128)S(1)}) fusion(f32[768]{0:T(1024)S(1)} %copy-done.15, bf16[3072,768]{1,0:T(8,128)(2,1)} %get-tuple-element.306, bf16[768,3072]{1,0:T(8,128)(2,1)} %get-tuple-element.304, f32[3072]{0:T(1024)S(1)} %copy-done.11, f32[512,768]{1,0:T(8,128)} %copy-done.1, f32[768]{0:T(1024)S(1)} %copy-done.14, ...), kind=kOutput, calls=%fused_computation.105.clone.1 | convolution fusion | flops 4940365312 | bytes 12610560 | tf_op jit(solution)/shard_map/while/body/eval_jaxpr/dot_general | solution.py:65
  410.3 1.2 fusion.133
  411.5 6.3 %copy.34 = bf16[8,512,768]{2,0,1:T(8,128)(2,1)S(1)} copy(bf16[8,512,768]{2,1,0:T(8,128)(2,1)} %get-tuple-element.89) | data formatting | bytes 12582912 | tf_op jit(solution)/shard_map/while | solution.py:106
  418.8 1.9 fusion.71
  421.5 43.0 %all-reduce = (f32[768]{0:T(1024)}, f32[768,3]{0,1:T(4,128)}, f32[3]{0:T(128)}, f32[]{:T(128)}, f32[]{:T(128)}) all-reduce(f32[768]{0:T(1024)S(1)} %get-tuple-element.143, f32[768,3]{0,1:T(4,128)S(1)} %fusion.81, f32[3]{0:T(128)S(1)} %get-tuple-element.129, ...), channel_id=1, replica_groups=mesh['wide'=8,'narrow'=4] {'wide','narrow'}, use_global_device_ids=true, to_apply=%region_12.13 | all-reduce | flops 3077 | bytes 24616 | tf_op jit(solution)/shard_map/psum | solution.py:125
  465.9 93.1 %all-reduce.3.cloned.1.call-done = f32[768,768]{1,0:T(8,128)} async-done(((f32[768,768]{1,0:T(8,128)}), f32[768,768]{1,0:T(8,128)}) %all-reduce.3.cloned.1.call-update) | async-done | bytes 2359312 | tf_op jit(solution)/shard_map/psum | solution.py:125
  559.0 3.2 copy.52
  (271 shorter events, 27.7 us)
Async XLA Ops:
  7.2 410.7 %copy-start = (bf16[768,768]{1,0:T(8,128)(2,1)S(1)}, bf16[768,768]{1,0:T(8,128)(2,1)}, u32[]{:S(2)}) copy-start(bf16[768,768]{1,0:T(8,128)(2,1)} %param.36) | copy-start | bytes 3538948
  7.2 551.8 %all-reduce.3.cloned.1.call-start = ((), (), s32[]{:S(2)}) async-start(), calls=%async_computation | async-start | bytes 4718592 | tf_op jit(solution)/shard_map/psum | solution.py:125
  25.4 6.0 %copy-start.10 = (bf16[768,768]{1,0:T(8,128)(2,1)S(1)}, bf16[768,768]{1,0:T(8,128)(2,1)}, u32[]{:S(2)}) copy-start(bf16[768,768]{1,0:T(8,128)(2,1)} %get-tuple-element.300) | copy-start | bytes 3538948 | tf_op jit(solution)/shard_map/while
  25.4 6.0 %copy-start.12 = (f32[768]{0:T(1024)S(1)}, f32[768]{0:T(1024)}, u32[]{:S(2)}) copy-start(f32[768]{0:T(1024)} %get-tuple-element.301) | copy-start | bytes 9220 | tf_op jit(solution)/shard_map/while
  31.3 3.3 copy-start.11
  31.3 3.3 copy-start.13
  31.3 3.3 copy-start.14
  34.6 22.1 %copy-start.2 = (f32[768]{0:T(1024)S(1)}, f32[768]{0:T(1024)}, u32[]{:S(2)}) copy-start(f32[768]{0:T(1024)} %get-tuple-element.308) | copy-start | bytes 9220 | tf_op jit(solution)/shard_map/while
  34.6 22.1 %copy-start.3 = (f32[768]{0:T(1024)S(1)}, f32[768]{0:T(1024)}, u32[]{:S(2)}) copy-start(f32[768]{0:T(1024)} %get-tuple-element.309) | copy-start | bytes 9220 | tf_op jit(solution)/shard_map/while
  75.9 6.0 %copy-start.10 = (bf16[768,768]{1,0:T(8,128)(2,1)S(1)}, bf16[768,768]{1,0:T(8,128)(2,1)}, u32[]{:S(2)}) copy-start(bf16[768,768]{1,0:T(8,128)(2,1)} %get-tuple-element.300) | copy-start | bytes 3538948 | tf_op jit(solution)/shard_map/while
  75.9 6.0 %copy-start.12 = (f32[768]{0:T(1024)S(1)}, f32[768]{0:T(1024)}, u32[]{:S(2)}) copy-start(f32[768]{0:T(1024)} %get-tuple-element.301) | copy-start | bytes 9220 | tf_op jit(solution)/shard_map/while
  81.8 3.3 copy-start.11
  81.8 3.3 copy-start.13
  81.8 3.3 copy-start.14
  85.1 22.1 %copy-start.2 = (f32[768]{0:T(1024)S(1)}, f32[768]{0:T(1024)}, u32[]{:S(2)}) copy-start(f32[768]{0:T(1024)} %get-tuple-element.308) | copy-start | bytes 9220 | tf_op jit(solution)/shard_map/while
  85.1 22.1 %copy-start.3 = (f32[768]{0:T(1024)S(1)}, f32[768]{0:T(1024)}, u32[]{:S(2)}) copy-start(f32[768]{0:T(1024)} %get-tuple-element.309) | copy-start | bytes 9220 | tf_op jit(solution)/shard_map/while
  126.4 6.0 %copy-start.10 = (bf16[768,768]{1,0:T(8,128)(2,1)S(1)}, bf16[768,768]{1,0:T(8,128)(2,1)}, u32[]{:S(2)}) copy-start(bf16[768,768]{1,0:T(8,128)(2,1)} %get-tuple-element.300) | copy-start | bytes 3538948 | tf_op jit(solution)/shard_map/while
  126.4 6.0 %copy-start.12 = (f32[768]{0:T(1024)S(1)}, f32[768]{0:T(1024)}, u32[]{:S(2)}) copy-start(f32[768]{0:T(1024)} %get-tuple-element.301) | copy-start | bytes 9220 | tf_op jit(solution)/shard_map/while
  132.3 3.3 copy-start.11
  132.3 3.3 copy-start.13
  132.3 3.3 copy-start.14
  135.6 22.1 %copy-start.2 = (f32[768]{0:T(1024)S(1)}, f32[768]{0:T(1024)}, u32[]{:S(2)}) copy-start(f32[768]{0:T(1024)} %get-tuple-element.308) | copy-start | bytes 9220 | tf_op jit(solution)/shard_map/while
  135.6 22.1 %copy-start.3 = (f32[768]{0:T(1024)S(1)}, f32[768]{0:T(1024)}, u32[]{:S(2)}) copy-start(f32[768]{0:T(1024)} %get-tuple-element.309) | copy-start | bytes 9220 | tf_op jit(solution)/shard_map/while
  176.9 6.0 %copy-start.10 = (bf16[768,768]{1,0:T(8,128)(2,1)S(1)}, bf16[768,768]{1,0:T(8,128)(2,1)}, u32[]{:S(2)}) copy-start(bf16[768,768]{1,0:T(8,128)(2,1)} %get-tuple-element.300) | copy-start | bytes 3538948 | tf_op jit(solution)/shard_map/while
  176.9 6.0 %copy-start.12 = (f32[768]{0:T(1024)S(1)}, f32[768]{0:T(1024)}, u32[]{:S(2)}) copy-start(f32[768]{0:T(1024)} %get-tuple-element.301) | copy-start | bytes 9220 | tf_op jit(solution)/shard_map/while
  182.8 3.3 copy-start.11
  182.8 3.3 copy-start.13
  182.9 3.3 copy-start.14
  186.1 22.1 %copy-start.2 = (f32[768]{0:T(1024)S(1)}, f32[768]{0:T(1024)}, u32[]{:S(2)}) copy-start(f32[768]{0:T(1024)} %get-tuple-element.308) | copy-start | bytes 9220 | tf_op jit(solution)/shard_map/while
  186.1 22.1 %copy-start.3 = (f32[768]{0:T(1024)S(1)}, f32[768]{0:T(1024)}, u32[]{:S(2)}) copy-start(f32[768]{0:T(1024)} %get-tuple-element.309) | copy-start | bytes 9220 | tf_op jit(solution)/shard_map/while
  227.4 6.0 %copy-start.10 = (bf16[768,768]{1,0:T(8,128)(2,1)S(1)}, bf16[768,768]{1,0:T(8,128)(2,1)}, u32[]{:S(2)}) copy-start(bf16[768,768]{1,0:T(8,128)(2,1)} %get-tuple-element.300) | copy-start | bytes 3538948 | tf_op jit(solution)/shard_map/while
  227.4 6.0 %copy-start.12 = (f32[768]{0:T(1024)S(1)}, f32[768]{0:T(1024)}, u32[]{:S(2)}) copy-start(f32[768]{0:T(1024)} %get-tuple-element.301) | copy-start | bytes 9220 | tf_op jit(solution)/shard_map/while
  233.3 3.3 copy-start.11
  233.4 3.3 copy-start.13
  233.4 3.3 copy-start.14
  236.6 22.1 %copy-start.2 = (f32[768]{0:T(1024)S(1)}, f32[768]{0:T(1024)}, u32[]{:S(2)}) copy-start(f32[768]{0:T(1024)} %get-tuple-element.308) | copy-start | bytes 9220 | tf_op jit(solution)/shard_map/while
  236.7 22.1 %copy-start.3 = (f32[768]{0:T(1024)S(1)}, f32[768]{0:T(1024)}, u32[]{:S(2)}) copy-start(f32[768]{0:T(1024)} %get-tuple-element.309) | copy-start | bytes 9220 | tf_op jit(solution)/shard_map/while
  277.9 6.0 %copy-start.10 = (bf16[768,768]{1,0:T(8,128)(2,1)S(1)}, bf16[768,768]{1,0:T(8,128)(2,1)}, u32[]{:S(2)}) copy-start(bf16[768,768]{1,0:T(8,128)(2,1)} %get-tuple-element.300) | copy-start | bytes 3538948 | tf_op jit(solution)/shard_map/while
  278.0 6.0 %copy-start.12 = (f32[768]{0:T(1024)S(1)}, f32[768]{0:T(1024)}, u32[]{:S(2)}) copy-start(f32[768]{0:T(1024)} %get-tuple-element.301) | copy-start | bytes 9220 | tf_op jit(solution)/shard_map/while
  283.9 3.3 copy-start.11
  283.9 3.3 copy-start.13
  283.9 3.3 copy-start.14
  287.2 22.1 %copy-start.2 = (f32[768]{0:T(1024)S(1)}, f32[768]{0:T(1024)}, u32[]{:S(2)}) copy-start(f32[768]{0:T(1024)} %get-tuple-element.308) | copy-start | bytes 9220 | tf_op jit(solution)/shard_map/while
  287.2 22.1 %copy-start.3 = (f32[768]{0:T(1024)S(1)}, f32[768]{0:T(1024)}, u32[]{:S(2)}) copy-start(f32[768]{0:T(1024)} %get-tuple-element.309) | copy-start | bytes 9220 | tf_op jit(solution)/shard_map/while
  328.5 6.0 %copy-start.10 = (bf16[768,768]{1,0:T(8,128)(2,1)S(1)}, bf16[768,768]{1,0:T(8,128)(2,1)}, u32[]{:S(2)}) copy-start(bf16[768,768]{1,0:T(8,128)(2,1)} %get-tuple-element.300) | copy-start | bytes 3538948 | tf_op jit(solution)/shard_map/while
  328.5 6.0 %copy-start.12 = (f32[768]{0:T(1024)S(1)}, f32[768]{0:T(1024)}, u32[]{:S(2)}) copy-start(f32[768]{0:T(1024)} %get-tuple-element.301) | copy-start | bytes 9220 | tf_op jit(solution)/shard_map/while
  334.4 3.3 copy-start.11
  334.4 3.3 copy-start.13
  334.4 3.3 copy-start.14
  337.7 22.1 %copy-start.2 = (f32[768]{0:T(1024)S(1)}, f32[768]{0:T(1024)}, u32[]{:S(2)}) copy-start(f32[768]{0:T(1024)} %get-tuple-element.308) | copy-start | bytes 9220 | tf_op jit(solution)/shard_map/while
  337.7 22.1 %copy-start.3 = (f32[768]{0:T(1024)S(1)}, f32[768]{0:T(1024)}, u32[]{:S(2)}) copy-start(f32[768]{0:T(1024)} %get-tuple-element.309) | copy-start | bytes 9220 | tf_op jit(solution)/shard_map/while
  379.0 6.0 %copy-start.10 = (bf16[768,768]{1,0:T(8,128)(2,1)S(1)}, bf16[768,768]{1,0:T(8,128)(2,1)}, u32[]{:S(2)}) copy-start(bf16[768,768]{1,0:T(8,128)(2,1)} %get-tuple-element.300) | copy-start | bytes 3538948 | tf_op jit(solution)/shard_map/while
  379.0 6.0 %copy-start.12 = (f32[768]{0:T(1024)S(1)}, f32[768]{0:T(1024)}, u32[]{:S(2)}) copy-start(f32[768]{0:T(1024)} %get-tuple-element.301) | copy-start | bytes 9220 | tf_op jit(solution)/shard_map/while
  384.9 3.3 copy-start.11
  384.9 3.3 copy-start.13
  384.9 3.3 copy-start.14
  388.2 22.1 %copy-start.2 = (f32[768]{0:T(1024)S(1)}, f32[768]{0:T(1024)}, u32[]{:S(2)}) copy-start(f32[768]{0:T(1024)} %get-tuple-element.308) | copy-start | bytes 9220 | tf_op jit(solution)/shard_map/while
  388.2 22.1 %copy-start.3 = (f32[768]{0:T(1024)S(1)}, f32[768]{0:T(1024)}, u32[]{:S(2)}) copy-start(f32[768]{0:T(1024)} %get-tuple-element.309) | copy-start | bytes 9220 | tf_op jit(solution)/shard_map/while
  411.5 6.4 %copy-start.6 = (f32[768]{0:T(1024)S(1)}, f32[768]{0:T(1024)}, u32[]{:S(2)}) copy-start(f32[768]{0:T(1024)} %param.37) | copy-start | bytes 9220
  411.5 6.7 %copy-start.4 = (f32[768,3]{0,1:T(4,128)S(1)}, f32[768,3]{0,1:T(4,128)}, u32[]{:S(2)}) copy-start(f32[768,3]{0,1:T(4,128)} %param.38) | copy-start | bytes 27652
  411.5 6.7 %copy-start.16 = (f32[3]{0:T(128)S(1)}, f32[3]{0:T(128)}, u32[]{:S(2)}) copy-start(f32[3]{0:T(128)} %param.39) | copy-start | bytes 40
  411.5 6.9 %copy-start.7 = (s32[8]{0:T(128)S(1)}, s32[8]{0:T(128)}, u32[]{:S(2)}) copy-start(s32[8]{0:T(128)} %param.23) | copy-start | bytes 100
  411.5 9.2 %copy-start.9 = (s32[8]{0:T(128)S(1)}, s32[8]{0:T(128)}, u32[]{:S(2)}) copy-start(s32[8]{0:T(128)} %get-tuple-element.322) | copy-start | bytes 100
  418.4 143.9 %copy-start.5 = (f32[8,3]{0,1:T(4,128)}, f32[8,3]{0,1:T(4,128)S(1)}, u32[]{:S(2)}) copy-start(f32[8,3]{0,1:T(4,128)S(1)} %get-tuple-element.312) | copy-start | bytes 292
  (24 other events, 48.2 us)
Sparse Core Ops, SparseCore 0:
  420.9 138.1 all-reduce.2
where the time goes:
time: 571 us; the launch traced here: 570 us
  matrix products  359 us (63%)
  waiting for transfers between devices  93.2 us (16%)
  blocking collectives  43 us (8%)
  local copies, waits for them, and re-layouts  36.4 us (6%)
  other arithmetic  20.5 us (4%)
  between operations  16.6 us (3%)
    dot_general x8, matrix products, encode(): jnp.dot(active, down_weight, preferred_element_type=jnp.float32) + down_bias  174 us
    psum x1, waiting for transfers between devices, local(): lax.psum((grad_pooler_weight, grad_ramp_weight, grad_pooler_bias, grad_ra...  93.1 us
    sub x8, matrix products, encode(): weights_exp = jnp.exp(scores - row_max)  85.2 us
    dot_general x8, matrix products, encode(): jnp.einsum('hqk,khd->qhd', attention, value_rows, preferred_element_type=...  47.1 us
    psum x1, blocking collectives, local(): lax.psum((grad_pooler_weight, grad_ramp_weight, grad_pooler_bias, grad_ra...  43 us
    dot_general x8, matrix products, encode(): jnp.dot(tokens, qkv_weight, preferred_element_type=jnp.float32) + qkv_bias  33.7 us
    dot_general x8, matrix products, encode(): jnp.dot(context, out_weight, preferred_element_type=jnp.float32) + out_bias  16.5 us
  transfers between devices with their start and end apart: 1, of which 1 were waited for; matrix products, arithmetic and copies ran while one was open for 0% of the time, Pallas kernels for 0%

commit v1 on v0

v1 whole, which is shorter than its diff:
```python
import functools

import jax
import jax.numpy as jnp
from jax import lax
from jax.experimental import pallas as pl
from jax.experimental.pallas import tpu as pltpu
from jax.sharding import PartitionSpec as P

D = 768
HEADS = 12
HEAD_DIM = 64
FF = 3072
CLASSES = 3
LANES = 128
PAIRS = HEADS // 2
KEY_BLOCK = 128
CHUNK = 512
EXTRA = 128

AXES = ("wide", "narrow")
HIGHEST = lax.Precision.HIGHEST
ROWS_BY_ROWS = (((1,), (1,)), ((), ()))
COLS_BY_COLS = (((0,), (0,)), ((), ()))
f32 = jnp.float32
bf16 = jnp.bfloat16


def layer_norm(values, gain, shift):
    center = values - jnp.mean(values, axis=-1, keepdims=True)
    spread = jnp.mean(center * center, axis=-1, keepdims=True)
    return center * lax.rsqrt(spread + 1e-12) * gain + shift


def gelu(values):
    half = 0.5 * values
    return half + half * lax.erf(values * 0.7071067811865476)


def project_keys(x_ref, slot, blocks, length, weight, bias, keys, values):
    rows = blocks * KEY_BLOCK
    tokens = x_ref[slot, :rows, :]
    visible = lax.broadcasted_iota(jnp.int32, (rows, 1), 0) < length
    key_rows = jnp.dot(tokens, weight[:, D : 2 * D], preferred_element_type=f32) + bias[:, D : 2 * D]
    keys[slot, :rows, :] = jnp.where(visible, key_rows, key_rows[0:1, :]).astype(bf16)
    value_rows = jnp.dot(tokens, weight[:, 2 * D :], preferred_element_type=f32) + bias[:, 2 * D :]
    values[slot, :rows, :] = jnp.where(visible, value_rows, 0.0).astype(bf16)


def attend(queries, keys, values, slot, blocks, length, context, row, rows):
    low = lax.broadcasted_iota(jnp.int32, (1, LANES), 1) < HEAD_DIM
    zero = jnp.zeros((), bf16)

    def apart(block):
        return jnp.concatenate([jnp.where(low, block, zero), jnp.where(low, zero, block)], axis=0)

    ones = apart(jnp.ones((KEY_BLOCK, LANES), bf16))
    last = (blocks - 1) * KEY_BLOCK + lax.broadcasted_iota(jnp.int32, (KEY_BLOCK, LANES), 0) < length
    ones_last = apart(jnp.where(last, 1.0, 0.0).astype(bf16))
    for pair in range(PAIRS):
        lanes = slice(pair * LANES, (pair + 1) * LANES)
        mine = queries[row : row + rows, lanes]
        scores = []
        for block in range(blocks):
            spot = slice(block * KEY_BLOCK, (block + 1) * KEY_BLOCK)
            scores.append(
                lax.dot_general(mine, apart(keys[slot, spot, lanes]), ROWS_BY_ROWS, preferred_element_type=f32)
            )
        top = functools.reduce(jnp.maximum, scores)
        top_low = jnp.max(top[:, :KEY_BLOCK], axis=-1, keepdims=True)
        top_high = jnp.max(top[:, KEY_BLOCK:], axis=-1, keepdims=True)
        total = None
        for block in range(blocks):
            spot = slice(block * KEY_BLOCK, (block + 1) * KEY_BLOCK)
            weights = jnp.concatenate(
                [
                    jnp.exp(scores[block][:, :KEY_BLOCK] - top_low).astype(bf16),
                    jnp.exp(scores[block][:, KEY_BLOCK:] - top_high).astype(bf16),
                ],
                axis=1,
            )
            held = jnp.concatenate(
                [apart(values[slot, spot, lanes]), ones_last if block == blocks - 1 else ones], axis=1
            )
            term = jnp.dot(weights, held, preferred_element_type=f32)
            total = term if total is None else total + term
        context[row : row + rows, lanes] = (total[:, :LANES] / total[:, LANES:]).astype(bf16)


def finish(tokens, context, out_w, up_w, down_w, biases, active):
    out_bias, attention_gain, attention_shift, up_bias, down_bias, output_gain, output_shift = biases
    attended = jnp.dot(context[...], out_w[...], preferred_element_type=f32) + out_bias[...]
    after = layer_norm(tokens.astype(f32) + attended, attention_gain[...], attention_shift[...])
    after_low = after.astype(bf16)
    for start in range(0, FF, CHUNK):
        spot = slice(start, start + CHUNK)
        expanded = jnp.dot(after_low, up_w[:, spot], preferred_element_type=f32) + up_bias[:, spot]
        active[:, spot] = gelu(expanded).astype(bf16)
    second = jnp.dot(active[...], down_w[...], preferred_element_type=f32) + down_bias[...]
    return layer_norm(after + second, output_gain[...], output_shift[...]).astype(bf16)


def first_kernel(
    half,
    lengths, labels,
    x_hbm, qkv_hbm, out_hbm, up_hbm, down_hbm,
    qkv_bias, *rest,
):
    biases = rest[:7]
    hidden_hbm, keys_hbm, values_hbm, lead = rest[7:11]
    x, qkv_w, out_w, up_w, down_w, keys, values, queries, context, active, result, load_sem, x_sem, store_sem, kv_sem = rest[11:]
    slots = x.shape[0]
    tiles = slots // 2

    def load_x(slot):
        return pltpu.make_async_copy(x_hbm.at[slot], x.at[slot], x_sem.at[slot])

    weights = [(qkv_hbm, qkv_w), (out_hbm, out_w), (up_hbm, up_w), (down_hbm, down_w)]
    loads = [pltpu.make_async_copy(a, b, load_sem.at[i]) for i, (a, b) in enumerate(weights)]

    def store(tile):
        return pltpu.make_async_copy(
            result.at[tile], hidden_hbm.at[pl.ds(2 * tile, 2), pl.ds(0, half), :], store_sem.at[tile]
        )

    def store_kv(slot):
        return (
            pltpu.make_async_copy(keys.at[slot], keys_hbm.at[slot], kv_sem.at[0, slot]),
            pltpu.make_async_copy(values.at[slot], values_hbm.at[slot], kv_sem.at[1, slot]),
        )

    for slot in range(2):
        load_x(slot).start()
    loads[0].start()
    for slot in range(2, slots):
        load_x(slot).start()
    for load in loads[1:]:
        load.start()
    loads[0].wait()

    def tile_step(tile, carry):
        for j in range(2):
            load_x(2 * tile + j).wait()
        tokens = x[pl.ds(2 * tile, 2), :half, :].reshape(2 * half, D)
        projected = jnp.dot(tokens, qkv_w[:, :D], preferred_element_type=f32) + qkv_bias[:, :D]
        queries[...] = projected.astype(bf16) * jnp.asarray(HEAD_DIM ** (-0.5), bf16)
        for j in range(2):
            slot = 2 * tile + j
            length = lengths[slot]
            count = (length + KEY_BLOCK - 1) // KEY_BLOCK
            for blocks in range(1, x.shape[1] // KEY_BLOCK + 1):

                @pl.when(count == blocks)
                def _():
                    project_keys(x, slot, blocks, length, qkv_w, qkv_bias, keys, values)
                    attend(queries, keys, values, slot, blocks, length, context, j * half, half)

            for copy in store_kv(slot):
                copy.start()

        @pl.when(tile == 0)
        def _():
            for load in loads[1:]:
                load.wait()

        done = finish(tokens, context, out_w, up_w, down_w, biases, active)
        result[tile] = done.reshape(2, half, D)
        for j in range(2):
            slot = 2 * tile + j
            place = lax.broadcasted_iota(jnp.int32, (1, EXTRA), 1)
            facts = jnp.where(place == 0, lengths[slot], labels[slot]).astype(f32)
            lead[pl.ds(slot, 1), :] = jnp.concatenate([done[j * half : j * half + 1, :].astype(f32), facts], axis=1)
        store(tile).start()
        return carry

    lax.fori_loop(0, tiles, tile_step, 0)
    for tile in range(tiles):
        store(tile).wait()
    for slot in range(slots):
        for copy in store_kv(slot):
            copy.wait()


def second_kernel(
    half,
    lengths,
    x_hbm, keys_hbm, values_hbm, qkv_hbm, out_hbm, up_hbm, down_hbm, hidden_in_place,
    qkv_bias, *rest,
):
    biases = rest[:7]
    (hidden_hbm,) = rest[7:8]
    x, q_w, out_w, up_w, down_w, keys, values, queries, context, active, result, load_sem, x_sem, store_sem, kv_sem = rest[8:]
    slots = x.shape[0]
    tiles = slots // 2

    def load_x(slot):
        return pltpu.make_async_copy(x_hbm.at[slot, pl.ds(half, half), :], x.at[slot], x_sem.at[slot])

    def load_kv(slot):
        return (
            pltpu.make_async_copy(keys_hbm.at[slot], keys.at[slot], kv_sem.at[0, slot]),
            pltpu.make_async_copy(values_hbm.at[slot], values.at[slot], kv_sem.at[1, slot]),
        )

    weights = [(qkv_hbm.at[:, pl.ds(0, D)], q_w), (out_hbm, out_w), (up_hbm, up_w), (down_hbm, down_w)]
    loads = [pltpu.make_async_copy(a, b, load_sem.at[i]) for i, (a, b) in enumerate(weights)]

    def store(tile):
        return pltpu.make_async_copy(
            result.at[tile], hidden_hbm.at[pl.ds(2 * tile, 2), pl.ds(half, half), :], store_sem.at[tile]
        )

    def load_slot(slot):
        load_x(slot).start()
        for copy in load_kv(slot):
            copy.start()

    for slot in range(2):
        load_x(slot).start()
    loads[0].start()
    for slot in range(2):
        for copy in load_kv(slot):
            copy.start()
    for load in loads[1:]:
        load.start()
    for slot in range(2, slots):
        load_slot(slot)
    loads[0].wait()

    def tile_step(tile, carry):
        for j in range(2):
            load_x(2 * tile + j).wait()
        tokens = x[pl.ds(2 * tile, 2), :, :].reshape(2 * half, D)
        projected = jnp.dot(tokens, q_w[...], preferred_element_type=f32) + qkv_bias[:, :D]
        queries[...] = projected.astype(bf16) * jnp.asarray(HEAD_DIM ** (-0.5), bf16)
        for j in range(2):
            slot = 2 * tile + j
            for copy in load_kv(slot):
                copy.wait()
            length = lengths[slot]
            count = (length + KEY_BLOCK - 1) // KEY_BLOCK
            for blocks in range(1, keys.shape[1] // KEY_BLOCK + 1):

                @pl.when(count == blocks)
                def _():
                    attend(queries, keys, values, slot, blocks, length, context, j * half, half)

        @pl.when(tile == 0)
        def _():
            for load in loads[1:]:
                load.wait()

        done = finish(tokens, context, out_w, up_w, down_w, biases, active)
        result[tile] = done.reshape(2, half, D)
        store(tile).start()
        return carry

    lax.fori_loop(0, tiles, tile_step, 0)
    for tile in range(tiles):
        store(tile).wait()


def ramp_kernel(gathered, pooler_w, pooler_b, ramp_w, ramp_b, logits_out, gpw_out, gpb_out, grw_out, grb_out, entropy_out, scored):
    own = logits_out.shape[0]
    leading = gathered[:, :D].astype(bf16)
    lengths = gathered[:, D : D + 1]
    labels = gathered[:, D + 1 : D + 2]
    pooled = jnp.tanh(jnp.dot(leading, pooler_w[...], preferred_element_type=f32) + pooler_b[...])
    logits = jnp.dot(pooled, ramp_w[...], precision=HIGHEST, preferred_element_type=f32) + ramp_b[...]
    scored[...] = logits
    wide, narrow = lax.axis_index(AXES[0]), lax.axis_index(AXES[1])
    place = wide * lax.axis_size(AXES[1]) + narrow
    logits_out[...] = scored[pl.ds(place * own, own), :]
    shifted = logits - jnp.max(logits, axis=1, keepdims=True)
    powers = jnp.exp(shifted)
    total = jnp.sum(powers, axis=1, keepdims=True)
    probs = powers / total
    classes = lax.broadcasted_iota(jnp.int32, logits.shape, 1).astype(f32)
    dlogits = probs - jnp.where(classes == labels, 1.0, 0.0)
    grw_out[...] = lax.dot_general(pooled, dlogits, COLS_BY_COLS, precision=HIGHEST, preferred_element_type=f32)
    grb_out[...] = jnp.sum(dlogits, axis=0, keepdims=True)
    back = lax.dot_general(dlogits, ramp_w[...], ROWS_BY_ROWS, precision=HIGHEST, preferred_element_type=f32)
    pooled_grad = (back * (1.0 - pooled * pooled)).astype(bf16)
    gpw_out[...] = lax.dot_general(leading, pooled_grad, COLS_BY_COLS, preferred_element_type=f32)
    gpb_out[...] = jnp.sum(pooled_grad.astype(f32), axis=0, keepdims=True)
    log_probs = shifted - jnp.log(total)
    row_entropy = -jnp.sum(jnp.exp(log_probs) * log_probs, axis=1, keepdims=True)
    entropy_out[...] = jnp.sum(lengths * row_entropy, axis=0, keepdims=True) / jnp.sum(lengths, axis=0, keepdims=True)


VMEM_LIMIT = 56 * 1024 * 1024


def local(
    hidden_in, lengths, labels,
    qkv_weight, qkv_bias, out_weight, out_bias, attention_gain, attention_shift,
    up_weight, up_bias, down_weight, down_bias, output_gain, output_shift,
    pooler_weight, pooler_bias, ramp_weight, ramp_bias,
):
    slots = lengths.shape[0]
    length = hidden_in.shape[0] // slots
    half = length // 2
    sequences = hidden_in.reshape(slots, length, D)
    row = lambda vector: vector.reshape(1, -1)
    biases = [row(v) for v in (qkv_bias, out_bias, attention_gain, attention_shift, up_bias, down_bias, output_gain, output_shift)]
    anywhere = pl.BlockSpec(memory_space=pl.ANY)
    scalars = pl.BlockSpec(memory_space=pltpu.SMEM)
    vmem = pl.BlockSpec(memory_space=pltpu.VMEM)
    dma = pltpu.SemaphoreType.DMA
    dense = 2 * slots * half * D * (2 * D + 2 * FF)
    attention = 2 * 2 * slots * half * length * D
    common = [
        pltpu.VMEM((2 * half, D), bf16),
        pltpu.VMEM((2 * half, D), bf16),
        pltpu.VMEM((2 * half, FF), bf16),
        pltpu.VMEM((slots // 2, 2, half, D), bf16),
        dma((4,)),
        dma((slots,)),
        dma((slots // 2,)),
        dma((2, slots)),
    ]
    weight_scratch = [pltpu.VMEM((D, D), bf16), pltpu.VMEM((D, FF), bf16), pltpu.VMEM((FF, D), bf16)]
    kv_shape = (slots, length, D)
    hidden, keys, values, lead = pl.pallas_call(
        functools.partial(first_kernel, half),
        name="first_half",
        out_shape=[
            jax.ShapeDtypeStruct(kv_shape, bf16),
            jax.ShapeDtypeStruct(kv_shape, bf16),
            jax.ShapeDtypeStruct(kv_shape, bf16),
            jax.ShapeDtypeStruct((slots, D + EXTRA), f32),
        ],
        in_specs=[scalars] * 2 + [anywhere] * 5 + [vmem] * 8,
        out_specs=[anywhere] * 3 + [vmem],
        scratch_shapes=[pltpu.VMEM(kv_shape, bf16), pltpu.VMEM((D, 3 * D), bf16)]
        + weight_scratch
        + [pltpu.VMEM(kv_shape, bf16)] * 2
        + common,
        compiler_params=pltpu.CompilerParams(vmem_limit_bytes=VMEM_LIMIT),
        cost_estimate=pl.CostEstimate(flops=dense + attention, bytes_accessed=50_000_000, transcendentals=0),
    )(lengths, labels, sequences, qkv_weight, out_weight, up_weight, down_weight, *biases)
    gathered = lax.all_gather(lead, AXES, axis=0, tiled=True)
    hidden = pl.pallas_call(
        functools.partial(second_kernel, half),
        name="second_half",
        out_shape=jax.ShapeDtypeStruct(kv_shape, bf16),
        in_specs=[scalars] + [anywhere] * 8 + [vmem] * 8,
        out_specs=anywhere,
        scratch_shapes=[pltpu.VMEM((slots, half, D), bf16), pltpu.VMEM((D, D), bf16)]
        + weight_scratch
        + [pltpu.VMEM(kv_shape, bf16)] * 2
        + common,
        input_output_aliases={8: 0},
        compiler_params=pltpu.CompilerParams(vmem_limit_bytes=VMEM_LIMIT),
        cost_estimate=pl.CostEstimate(flops=dense + attention, bytes_accessed=50_000_000, transcendentals=0),
    )(lengths, sequences, keys, values, qkv_weight, out_weight, up_weight, down_weight, hidden, *biases)
    one = lambda *shape: jax.ShapeDtypeStruct(shape, f32)
    logits, gpw, gpb, grw, grb, entropy = pl.pallas_call(
        ramp_kernel,
        name="off_ramp",
        out_shape=[one(slots, CLASSES), one(D, D), one(1, D), one(D, CLASSES), one(1, CLASSES), one(1, 1)],
        in_specs=[vmem] * 5,
        out_specs=[vmem] * 6,
        scratch_shapes=[pltpu.VMEM((gathered.shape[0], CLASSES), f32)],
        compiler_params=pltpu.CompilerParams(vmem_limit_bytes=VMEM_LIMIT),
    )(gathered, pooler_weight, row(pooler_bias), ramp_weight, row(ramp_bias))
    return (
        hidden.reshape(hidden_in.shape),
        logits,
        gpw,
        gpb.reshape(D),
        grw,
        grb.reshape(CLASSES),
        entropy.reshape(()),
    )


def solution(mesh):
    spread = P(AXES)
    placed = (P(AXES, None), spread, spread) + (P(),) * 16
    return jax.shard_map(
        local,
        mesh=mesh,
        in_specs=placed,
        out_specs=(P(AXES, None), P(AXES, None), P(), P(), P(), P(), P()),
        check_vma=False,
    )
```

time: 571 us -> 229 us (0.40)
  matrix products: 359 us -> 0 us
  Pallas kernels: 0 us -> 119 us
  waiting for transfers between devices: 93.2 us -> 0 us
  blocking collectives: 43 us -> 95.3 us
  local copies, waits for them, and re-layouts: 36.4 us -> 13.6 us
  other arithmetic: 20.5 us -> 1.28 us
  between operations: 16.6 us -> 0.98 us
    dot_general x37 -> x0, matrix products: 274 us -> none  [the longest x8 174 us: encode(): jnp.dot(active, down_weight, preferred_element_type=jnp.float32) + down_bias]
    pallas_call x0 -> x3, Pallas kernels: none -> 119 us  [the longest x1 62.8 us: local(): pl.pallas_call(functools.partial(first_kernel, half), name='first_half',...]
    all_gather x0 -> x1, blocking collectives: none -> 95.3 us  [local(): gathered = lax.all_gather(lead, AXES, axis=0, tiled=True)]
    psum x1 -> x0, waiting for transfers between devices: 93.1 us -> none  [local(): lax.psum((grad_pooler_weight, grad_ramp_weight, grad_pooler_bias, grad_ra...]
    sub x8 -> x0, matrix products: 85.2 us -> none  [encode(): weights_exp = jnp.exp(scores - row_max)]
    psum x1 -> x0, blocking collectives: 43 us -> none  [local(): lax.psum((grad_pooler_weight, grad_ramp_weight, grad_pooler_bias, grad_ra...]
    slice x32 -> x0, local copies, waits for them, and re-layouts: 15 us -> none  [the longest x8 9.32 us: encode(): projected[:, :D].astype(jnp.bfloat16).reshape(rows, HEADS, HEAD_DIM)]
    while x161 -> x0, local copies, waits for them, and re-layouts: 13.4 us -> none
  transfers between devices with their start and end apart: 1 -> 0, of which waited for: 1 -> 0; matrix products, arithmetic and copies ran while one was open for 0% -> 0% of each run, Pallas kernels for 0% -> 0%
where the time goes in v1:
time: 229 us; the launch traced here: 230 us
  Pallas kernels  119 us (52%)
  blocking collectives  95.3 us (42%)
  local copies, waits for them, and re-layouts  13.6 us (6%)
    all_gather x1, blocking collectives, local(): gathered = lax.all_gather(lead, AXES, axis=0, tiled=True)  95.3 us
    pallas_call x1, Pallas kernels, local(): pl.pallas_call(functools.partial(first_kernel, half), name='first_half',...  62.8 us
    pallas_call x1, Pallas kernels, local(): pl.pallas_call(functools.partial(second_kernel, half), name='second_half'...  48.7 us
    reshape x8, local copies, waits for them, and re-layouts, local(): row = lambda vector: vector.reshape(1, -1)  9.56 us
    pallas_call x1, Pallas kernels, local(): pl.pallas_call(ramp_kernel, name='off_ramp', out_shape=[one(slots, CLASSE...  7.06 us

profile of v1, /device:TPU:0, one launch (start us, length us, event | category | flops | bytes accessed | tf_op | source)
XLA Modules:
  0.0 229.8 jit_solution(897995943774387455)
XLA Ops:
  0.6 1.3 reshape.60.qkv_bias
  1.9 1.3 reshape.61.rest_0_
  3.2 1.3 reshape.62.rest_1_
  4.5 1.3 reshape.63.rest_2_
  5.8 1.3 reshape.65.rest_4_
  7.0 1.3 reshape.66.rest_5_
  8.3 1.3 reshape.67.rest_6_
  9.6 62.8 %first_half.1 = (bf16[8,512,768]{2,1,0:T(8,128)(2,1)}, bf16[8,512,768]{2,1,0:T(8,128)(2,1)}, bf16[8,512,768]{2,1,0:T(8,128)(2,1)}, f32[8,896]{1,0:T(8,128)}) custom-call(s32[8]{0:T(128)} %lengths.3, s32[8]{0:T(128)} %labels.1, bf16[8,512,768]{2,1,0:T(8,128)(2,1)} %bitcast.7, bf16[768,2304]{1,0:T(8,128)(2,1)} %qkv_hbm.3, bf16[768,768]{1,0:T(8,128)(2,1)} %out_hbm.3, ...), custom_call_target="tpu_custom_call" | custom-call | flops 27380416512 | bytes 50000000 | tf_op jit(solution)/shard_map/first_half/pallas_call | solution.py:324
  72.5 0.0 copy-start
  72.5 0.0 copy-start.1
  72.5 0.0 copy-start.2
  72.5 48.7 %second_half.1 = bf16[8,512,768]{2,1,0:T(8,128)(2,1)} custom-call(s32[8]{0:T(128)} %lengths.3, bf16[8,512,768]{2,1,0:T(8,128)(2,1)} %bitcast.8, bf16[8,512,768]{2,1,0:T(8,128)(2,1)} %get-tuple-element.17.keys_hbm, bf16[8,512,768]{2,1,0:T(8,128)(2,1)} %get-tuple-element.18.values_hbm, bf16[768,2304]{1,0:T(8,128)(2,1)} %qkv_hbm.3, ...), custom_call_target="tpu_custom_call", output_to_operand_aliasing={{}: (8, {})} | custom-call | flops 27380416512 | bytes 50000000 | tf_op jit(solution)/shard_map/second_half/pallas_call | solution.py:343
  121.2 0.0 copy-done
  121.2 95.3 %all_gather.3.gathered = f32[256,896]{1,0:T(8,128)} all-gather(f32[8,896]{1,0:T(8,128)S(1)} %copy-done), channel_id=1, replica_groups=mesh['wide'=8,'narrow'=4] {'wide','narrow'}, dimensions={0}, use_global_device_ids=true | all-gather | bytes 946176 | tf_op jit(solution)/shard_map/all_gather | solution.py:342
  216.6 0.0 copy-done.1
  216.6 1.0 copy.27.ramp_w
  217.5 0.0 copy-done.2
  217.5 0.6 reshape.69.pooler_b
  218.1 7.1 %off_ramp.1 = (f32[8,3]{1,0:T(8,128)}, f32[768,768]{1,0:T(8,128)}, f32[1,768]{1,0:T(1,128)}, f32[768,3]{1,0:T(8,128)}, f32[1,3]{1,0:T(1,128)}, /*index=5*/f32[1,1]{1,0:T(1,128)}) custom-call(f32[256,896]{1,0:T(8,128)} %all_gather.3.gathered, bf16[768,768]{1,0:T(8,128)(2,1)} %pooler_w.1, f32[1,768]{1,0:T(1,128)} %reshape.69.pooler_b, f32[768,3]{1,0:T(8,128)} %copy.27.ramp_w, ...), custom_call_target="tpu_custom_call" | custom-call | tf_op jit(solution)/shard_map/off_ramp/pallas_call | solution.py:358
  225.2 1.7 copy.29
  226.9 1.3 reduce
  228.2 1.3 copy.28
Async XLA Ops:
  72.5 48.8 %copy-start = (f32[8,896]{1,0:T(8,128)S(1)}, f32[8,896]{1,0:T(8,128)}, u32[]{:S(2)}) copy-start(f32[8,896]{1,0:T(8,128)} %get-tuple-element.20) | copy-start | bytes 86020
  72.5 144.1 %copy-start.1 = (f32[768,3]{0,1:T(4,128)S(1)}, f32[768,3]{0,1:T(4,128)}, u32[]{:S(2)}) copy-start(f32[768,3]{0,1:T(4,128)} %param.36) | copy-start | bytes 27652
  72.5 145.1 %copy-start.2 = (f32[768]{0:T(1024)S(1)}, f32[768]{0:T(1024)}, u32[]{:S(2)}) copy-start(f32[768]{0:T(1024)} %param.35) | copy-start | bytes 9220
